TPU v7x, 32 devices: a whole 2x2x4 slice. The times are simulated.
32 devices in a mesh: dp: 16 (over z, y, x), tensor: 2 (over core).
Axes of the slice: x: 2, y: 2, z: 4, core: 2. Of those that a mesh axis runs over, the one named last changes fastest.
Arguments:
- activations: bfloat16 [4096, 53248], P('dp', 'tensor'), may hold values from -32 to 32
- test_matrix: bfloat16 [53248, 256], P('tensor', 'dp'), may hold values from -0.02734375 to 0.02734375
- gradient: bfloat16 [53248, 8192], P('tensor', 'dp'), may hold values from -16 to 16
Outputs:
- preconditioned: bfloat16 [53248, 8192], P('tensor', 'dp')
- gram_matrix: float32 [256, 256], replicated
All inputs are finite; a program needn't handle non-finite values.
Results may differ from a plain program's by a relative error of at most 0.0034.
Values may be sent and summed in bfloat16 or wider, within the bound.
No kernel may reach another device: no remote copies, remote signals or barrier semaphores. Data moves between devices by JAX's collectives and lax.ppermute only.
A program may use at most 192 MiB of HBM per device.

v0:
```python
import jax
import jax.numpy as jnp
from jax import lax
from jax.sharding import PartitionSpec as P

damping_ratio = 0.1


def symmetric(matrix):
    return 0.5 * (matrix + matrix.T)


def local(activations, test_matrix, gradient):
    dp_count = lax.axis_size("dp")
    tokens = activations.shape[0] * dp_count
    probe_full = lax.all_gather(test_matrix, "dp", axis=1, tiled=True)
    rank_size = probe_full.shape[1]
    partial_sketch = jnp.dot(activations, probe_full, preferred_element_type=jnp.float32)
    sketch = lax.psum(partial_sketch, "tensor")
    sketch_low = sketch.astype(jnp.bfloat16)
    exchanged = lax.all_to_all(activations, "dp", split_axis=1, concat_axis=0, tiled=True)
    sketch_all = lax.all_gather(sketch_low, "dp", axis=0, tiled=True)
    factor = (
        lax.dot_general(
            exchanged, sketch_all, (((0,), (0,)), ((), ())), preferred_element_type=jnp.float32
        )
        / tokens
    )
    local_core = jnp.dot(sketch.T, sketch_low.astype(jnp.float32), precision=lax.Precision.HIGHEST)
    core_matrix = symmetric(lax.psum(local_core, "dp") / tokens)
    chol_lower = jnp.linalg.cholesky(core_matrix)
    basis_local = jax.scipy.linalg.solve_triangular(chol_lower, factor.T, lower=True).T
    local_gram = jnp.dot(basis_local.T, basis_local, precision=lax.Precision.HIGHEST)
    gram_matrix = lax.psum(local_gram, ("dp", "tensor"))
    damping = damping_ratio * jnp.trace(gram_matrix) / rank_size
    kernel_lower = jnp.linalg.cholesky(
        gram_matrix + damping * jnp.eye(rank_size, dtype=jnp.float32)
    )
    basis_low = basis_local.astype(jnp.bfloat16)
    basis_all = lax.all_gather(basis_low, "dp", axis=0, tiled=True)
    projected_part = lax.dot_general(
        basis_all, gradient, (((0,), (0,)), ((), ())), preferred_element_type=jnp.float32
    )
    projected = lax.psum(projected_part, "tensor")
    weights = jax.scipy.linalg.cho_solve((kernel_lower, True), projected).astype(jnp.bfloat16)
    correction = jnp.dot(basis_all, weights, preferred_element_type=jnp.float32)
    return ((gradient.astype(jnp.float32) - correction).astype(jnp.bfloat16), gram_matrix)


def solution(mesh):
    placed = (P("dp", "tensor"), P("tensor", "dp"), P("tensor", "dp"))
    return jax.shard_map(
        local, mesh=mesh, in_specs=placed, out_specs=(P("tensor", "dp"), P()), check_vma=False
    )
```

profile of v0, /device:TPU:0, one launch (start us, length us, event | category | flops | bytes accessed | tf_op | source)
XLA Modules:
  0.0 1024.2 jit_solution(17857298710190046540)
XLA Ops:
  7.9 18.5 %copy.37 = bf16[256,26624]{0,1:T(8,128)(2,1)} copy(bf16[256,26624]{1,0:T(8,128)(2,1)} %param.4) | data formatting | bytes 27262976 | tf_op args[0]
  26.4 8.4 all-to-all-start
  34.8 379.8 %all-gather.4.cloned.1.call-done = bf16[26624,256]{0,1:T(8,128)(2,1)} async-done(((bf16[26624,16]{0,1:T(8,128)(2,1)}), bf16[26624,256]{0,1:T(8,128)(2,1)}) %all-gather.4.cloned.1.call-update) | async-done | bytes 13631504 | tf_op jit(solution)/shard_map/all_gather | solution.py:16
  414.6 13.2 %fusion.32 = f32[256,256]{1,0:T(8,128)} fusion(bf16[256,26624]{1,0:T(8,128)(2,1)} %param.4, bf16[26624,256]{0,1:T(8,128)(2,1)} %all-gather.4.cloned.1.call-done), kind=kOutput, calls=%fused_computation.76 | convolution fusion | flops 3489660928 | bytes 27525120 | tf_op jit(solution)/shard_map/dot_general | solution.py:18
  427.9 34.4 %all-reduce.6.cloned.1.call-done = f32[256,256]{1,0:T(8,128)} async-done(((f32[256,256]{1,0:T(8,128)}), f32[256,256]{1,0:T(8,128)}) %all-reduce.6.cloned.1.call-update) | async-done | bytes 262160 | tf_op jit(solution)/shard_map/psum | solution.py:19
  462.2 2.1 fusion.21
  464.4 1.6 convert_element_type.19
  466.3 18.0 %copy.38 = bf16[16,256,1664]{2,1,0:T(8,128)(2,1)} copy(bf16[16,256,1664]{1,2,0:T(8,128)(2,1)} %bitcast.6) | data formatting | bytes 27262976 | tf_op jit(solution)/shard_map/all_to_all | solution.py:21
  484.4 92.4 %all-reduce.8.cloned.1.call-done = f32[256,256]{1,0:T(8,128)} async-done(((f32[256,256]{1,0:T(8,128)}), f32[256,256]{1,0:T(8,128)}) %all-reduce.8.cloned.1.call-update) | async-done | bytes 262160 | tf_op jit(solution)/shard_map/psum | solution.py:30
  579.1 11.7 %cholesky.130 = f32[128,128]{1,0:T(8,128)S(1)} custom-call(f32[128,128]{1,0:T(8,128)S(1)} %cholesky.194), custom_call_target="Cholesky" | custom-call | tf_op jit(solution)/shard_map/jit(cholesky)/cholesky | solution.py:31
  590.9 9.8 custom-call.22
  601.3 11.7 %cholesky.147 = f32[128,128]{1,0:T(8,128)S(1)} custom-call(f32[128,128]{1,0:T(8,128)S(1)} %convolution_subtract_fusion.4), custom_call_target="Cholesky" | custom-call | tf_op jit(solution)/shard_map/jit(cholesky)/cholesky | solution.py:31
  615.3 4.2 while.2
  615.9 1.4 dynamic-slice.13
  618.0 1.4 dynamic-slice.13
  619.5 19.9 %custom-call.19 = f32[2,128,128]{1,2,0:T(8,128)S(1)} custom-call(f32[2,128,128]{2,1,0:T(8,128)S(1)} %get-tuple-element.10), custom_call_target="InvertDiagBlocksLowerTriangular" | custom-call | tf_op jit(solution)/shard_map/jit(_solve_triangular)/triangular_solve | solution.py:32
  639.9 8.5 convolution_multiply_fusion
  651.2 2.4 fusion
  655.1 122.2 %all-reduce.10.cloned.1.call-done = f32[256,256]{0,1:T(8,128)} async-done(((f32[256,256]{0,1:T(8,128)}), f32[256,256]{0,1:T(8,128)}) %all-reduce.10.cloned.1.call-update) | async-done | bytes 262160 | tf_op jit(solution)/shard_map/psum | solution.py:34
  777.3 1.6 select_reduce_fusion
  781.7 11.7 %cholesky.164 = f32[128,128]{1,0:T(8,128)S(1)} custom-call(f32[128,128]{1,0:T(8,128)S(1)} %cholesky.197), custom_call_target="Cholesky" | custom-call | tf_op jit(solution)/shard_map/jit(cholesky)/cholesky | solution.py:36
  793.5 9.8 custom-call.23
  803.9 11.7 %cholesky.181 = f32[128,128]{1,0:T(8,128)S(1)} custom-call(f32[128,128]{1,0:T(8,128)S(1)} %convolution_subtract_fusion.3), custom_call_target="Cholesky" | custom-call | tf_op jit(solution)/shard_map/jit(cholesky)/cholesky | solution.py:36
  818.4 124.4 %all-gather.8.cloned.1.call-done = bf16[26624,256]{0,1:T(8,128)(2,1)} async-done(((bf16[1664,256]{0,1:T(8,128)(2,1)}), bf16[26624,256]{0,1:T(8,128)(2,1)}) %all-gather.8.cloned.1.call-update) | async-done | bytes 13631504 | tf_op jit(solution)/shard_map/all_gather | solution.py:40
  942.8 17.2 %fusion.33 = f32[256,512]{1,0:T(8,128)} fusion(bf16[26624,256]{0,1:T(8,128)(2,1)} %all-gather.8.cloned.1.call-done, bf16[26624,512]{1,0:T(8,128)(2,1)} %param.6), kind=kOutput, calls=%fused_computation.77 | convolution fusion | flops 6979321856 | bytes 41418752 | tf_op jit(solution)/shard_map/dot_general | solution.py:41
  960.1 4.3 while.3
  960.7 1.4 dynamic-slice.15
  962.8 1.4 dynamic-slice.15
  964.4 19.7 %custom-call.20 = f32[2,128,128]{1,2,0:T(8,128)S(1)} custom-call(f32[2,128,128]{2,1,0:T(8,128)S(1)} %get-tuple-element.18), custom_call_target="InvertDiagBlocksLowerTriangular" | custom-call | tf_op jit(solution)/shard_map/jit(_cho_solve)/triangular_solve | solution.py:45
  984.9 1.4 fusion.5
  986.3 1.4 convolution_subtract_fusion.2
  989.2 28.0 %subtract_convert_fusion = bf16[26624,512]{1,0:T(8,128)(2,1)} fusion(bf16[26624,512]{1,0:T(8,128)(2,1)} %param.6, bf16[26624,256]{0,1:T(8,128)(2,1)} %all-gather.8.cloned.1.call-done, bf16[128,512]{1,0:T(8,128)(2,1)S(1)} %get-tuple-element.73, bf16[128,512]{1,0:T(8,128)(2,1)S(1)} %convolution_convert_fusion), kind=kOutput, calls=%fused_computation.4 | convolution fusion | flops 7020740608 | bytes 68419584 | tf_op jit(solution)/shard_map/dot_general | solution.py:46
  (83 shorter events, 19.2 us)
Async XLA Ops:
  7.2 407.5 %all-gather.4.cloned.1.call-start = ((), (), s32[]{:S(2)}) async-start(), calls=%async_computation.1 | async-start | bytes 14483456 | tf_op jit(solution)/shard_map/all_gather | solution.py:16
  26.4 440.0 %all-to-all-start = ((bf16[256,16,1664]{0,2,1:T(8,128)(2,1)}), bf16[256,16,1664]{0,2,1:T(8,128)(2,1)}, u32[]{:S(2)}, u32[]{:S(2)}) async-start(bf16[256,16,1664]{0,2,1:T(8,128)(2,1)} %bitcast.83), calls=%async_computation | async-start | bytes 27262976 | tf_op jit(solution)/shard_map/all_to_all | solution.py:21
  34.7 427.5 %all-reduce.6.cloned.1.call-start = ((), (), s32[]{:S(2)}) async-start(), calls=%async_computation.2 | async-start | bytes 524288 | tf_op jit(solution)/shard_map/psum | solution.py:19
  427.8 149.0 %all-reduce.8.cloned.1.call-start = ((), (), s32[]{:S(2)}) async-start(), calls=%async_computation.3 | async-start | bytes 524288 | tf_op jit(solution)/shard_map/psum | solution.py:30
  464.4 175.5 %all-gather.6.cloned.1.call-start = ((), (), s32[]{:S(2)}) async-start(), calls=%async_computation.4 | async-start | bytes 2228224 | tf_op jit(solution)/shard_map/all_gather | solution.py:22
  466.1 311.2 %all-reduce.10.cloned.1.call-start = ((), (), s32[]{:S(2)}) async-start(), calls=%async_computation.6 | async-start | bytes 524288 | tf_op jit(solution)/shard_map/psum | solution.py:34
  653.6 289.3 %all-gather.8.cloned.1.call-start = ((), (), s32[]{:S(2)}) async-start(), calls=%async_computation.5 | async-start | bytes 14483456 | tf_op jit(solution)/shard_map/all_gather | solution.py:40
  654.6 330.3 %all-reduce.12.cloned.1.call-start = ((), (), s32[]{:S(2)}) async-start(), calls=%async_computation.7 | async-start | bytes 1048576 | tf_op jit(solution)/shard_map/psum | solution.py:44
  818.4 165.7 %copy-start = (f32[256,256]{0,1:T(8,128)S(1)}, f32[256,256]{0,1:T(8,128)}, u32[]{:S(2)}) copy-start(f32[256,256]{0,1:T(8,128)} %all-reduce.10.cloned.1.call-done) | copy-start | bytes 786436
Sparse Core Ops, SparseCore 0:
  10.7 403.8 all-gather.3
  427.9 34.2 all-reduce.5
  468.9 107.8 all-reduce.7
  579.4 60.4 all-gather.5
  653.7 123.6 all-reduce.9
  780.5 162.3 all-gather.7
  960.2 17.1 all-reduce.11
where the time goes:
time: 1030 us; the launch traced here: 1020 us
  waiting for transfers between devices  755 us (73%)
  other arithmetic  116 us (11%)
  matrix products  79.2 us (8%)
  local copies, waits for them, and re-layouts  46.8 us (5%)
  between operations  17.8 us (2%)
    all_gather x1, waiting for transfers between devices, local(): probe_full = lax.all_gather(test_matrix, 'dp', axis=1, tiled=True)  380 us
    all_gather x1, waiting for transfers between devices, local(): basis_all = lax.all_gather(basis_low, 'dp', axis=0, tiled=True)  124 us
    psum x1, waiting for transfers between devices, local(): gram_matrix = lax.psum(local_gram, ('dp', 'tensor'))  122 us
    psum x1, waiting for transfers between devices, local(): core_matrix = symmetric(lax.psum(local_core, 'dp') / tokens)  92.4 us
    another operation x7, other arithmetic, local(): jnp.linalg.cholesky(gram_matrix + damping * jnp.eye(rank_size, dtype=jnp....  34.6 us
    psum x1, waiting for transfers between devices, local(): sketch = lax.psum(partial_sketch, 'tensor')  34.4 us
    another operation x6, other arithmetic, local(): chol_lower = jnp.linalg.cholesky(core_matrix)  34 us
    dot_general x1, matrix products, local(): correction = jnp.dot(basis_all, weights, preferred_element_type=jnp.float32)  28 us
  transfers between devices with their start and end apart: 8, of which 6 were waited for; matrix products, arithmetic and copies ran while one was open for 18% of the time, Pallas kernels for 0%

commit v1 on v0

v1 whole, which is shorter than its diff:
```python
import jax
import jax.numpy as jnp
from jax import lax
from jax.experimental import pallas as pl
from jax.experimental.pallas import tpu as pltpu
from jax.sharding import PartitionSpec as P

damping_ratio = 0.1
exact = lax.Precision.HIGHEST
megabyte = 1024 * 1024


def mul(a, b, dims=((1,), (0,))):
    return lax.dot_general(a, b, (dims, ((), ())), precision=exact, preferred_element_type=jnp.float32)


def low_mul(a, b, dims=((1,), (0,))):
    return lax.dot_general(a, b, (dims, ((), ())), preferred_element_type=jnp.float32)


def across(value, bit):
    count = lax.axis_size("dp")
    return lax.ppermute(value, "dp", [(i, i ^ bit) for i in range(count)])


def total_tensor(value):
    if lax.axis_size("tensor") == 2:
        return value + lax.ppermute(value, "tensor", [(0, 1), (1, 0)])
    return lax.psum(value, "tensor")


def round_end(*values):
    return lax.optimization_barrier(values)


def places(bits):
    found = [0]
    for bit in bits:
        found = found + [i ^ bit for i in found]
    return found


def send_half(piece, bit):
    half = piece.shape[0] // 2
    arrived = across(piece[half:], bit)
    return (piece[:half].astype(jnp.float32) + arrived.astype(jnp.float32)).astype(piece.dtype)


def small_inverse(block):
    side = block.shape[0]
    rows = lax.broadcasted_iota(jnp.int32, (side, 1), 0)
    lanes = lax.broadcasted_iota(jnp.int32, (side, side), 1)
    eye = (lax.broadcasted_iota(jnp.int32, (side, side), 0) == lanes).astype(jnp.float32)
    work = jnp.concatenate([block, eye], axis=1)
    scale = jnp.zeros((side, 1), jnp.float32)
    for j in range(side):
        row = work[j : j + 1, :]
        pivot = row[:, j : j + 1]
        scale = jnp.where(rows == j, lax.rsqrt(pivot), scale)
        work = work - jnp.where(rows > j, work[:, j : j + 1], 0.0) * (row * (1.0 / pivot))
    return work[:, side:] * scale


def lower_inverse_kernel(matrix_ref, out_ref, left_ref):
    size = matrix_ref.shape[0]
    side = min(64, size)
    out_ref[...] = jnp.zeros(out_ref.shape, jnp.float32)
    left_ref[...] = matrix_ref[...]
    for k in range(0, size, side):
        own = pl.ds(k, side)
        block = small_inverse(left_ref[own, k : k + side])
        if k:
            out_ref[own, :k] = -mul(block, mul(left_ref[own, :k], out_ref[:k, :k]))
        out_ref[own, k : k + side] = block
        if k + side < size:
            rest = pl.ds(k + side, size - k - side)
            lower = mul(left_ref[rest, k : k + side], block, ((1,), (1,)))
            left_ref[rest, k : k + side] = lower
            left_ref[rest, k + side :] = left_ref[rest, k + side :] - mul(lower, lower, ((1,), (1,)))


def lower_inverse(matrix):
    return pl.pallas_call(
        lower_inverse_kernel,
        out_shape=jax.ShapeDtypeStruct(matrix.shape, jnp.float32),
        scratch_shapes=[pltpu.VMEM(matrix.shape, jnp.float32)],
        compiler_params=pltpu.CompilerParams(vmem_limit_bytes=16 * megabyte),
        cost_estimate=pl.CostEstimate(flops=10**8, bytes_accessed=10**6, transcendentals=0),
        name="lower_inverse",
    )(matrix)


def chosen(activations, depth, rels, start, size):
    me = lax.axis_index("dp")
    own = activations.shape[0]
    source = jnp.asarray(rels, jnp.int32) ^ me
    if depth % 128 or size % 128:
        blocks = activations.reshape(own, -1, depth)[:, :, start : start + size]
        return jnp.take(blocks, source, axis=1).transpose(1, 0, 2)

    def kernel(source_ref, block_ref, out_ref):
        out_ref[0] = block_ref[:, start : start + size]

    return pl.pallas_call(
        kernel,
        grid_spec=pltpu.PrefetchScalarGridSpec(
            num_scalar_prefetch=1,
            grid=(len(rels),),
            in_specs=[pl.BlockSpec((own, depth), lambda i, source_ref: (0, source_ref[i]))],
            out_specs=pl.BlockSpec((1, own, size), lambda i, source_ref: (i, 0, 0)),
        ),
        out_shape=jax.ShapeDtypeStruct((len(rels), own, size), activations.dtype),
        compiler_params=pltpu.CompilerParams(vmem_limit_bytes=16 * megabyte),
        cost_estimate=pl.CostEstimate(flops=0, bytes_accessed=12 * 10**6, transcendentals=0),
        name="chosen",
    )(source, activations)


def partials(left, activations, depth, rels, cuts, orders, paired=None):
    me = lax.axis_index("dp")
    own = activations.shape[0]
    rank = left.shape[0]
    if depth % 128 or any(size % 128 for _, size in cuts):
        outs = []
        for (start, size), order in zip(cuts, orders):
            rows = chosen(activations, depth, [rels[p] for p in order], start, size)
            term = jnp.einsum("kt,rtb->rkb", left, rows, preferred_element_type=jnp.float32)
            if paired is not None:
                term = term + jnp.einsum("kt,rtb->rkb", paired[0], paired[1][jnp.asarray(order)], preferred_element_type=jnp.float32)
            outs.append(term.astype(jnp.bfloat16))
        return outs
    source = jnp.asarray(rels, jnp.int32) ^ me
    goes = jnp.asarray([[order.index(i) for i in range(len(rels))] for order in orders], jnp.int32)

    def kernel(source_ref, goes_ref, left_ref, block_ref, *refs):
        if paired is not None:
            other_left_ref, other_ref, *out_refs = refs
        else:
            out_refs = refs
        for (start, size), out_ref in zip(cuts, out_refs):
            term = jnp.dot(left_ref[...], block_ref[:, start : start + size], preferred_element_type=jnp.float32)
            if paired is not None:
                term = term + jnp.dot(other_left_ref[...], other_ref[0], preferred_element_type=jnp.float32)
            out_ref[0] = term.astype(out_ref.dtype)

    def out_spec(c, size):
        return pl.BlockSpec((1, rank, size), lambda i, source_ref, goes_ref: (goes_ref[c, i], 0, 0))

    in_specs = [
        pl.BlockSpec(left.shape, lambda i, source_ref, goes_ref: (0, 0)),
        pl.BlockSpec((own, depth), lambda i, source_ref, goes_ref: (0, source_ref[i])),
    ]
    operands = [left, activations]
    if paired is not None:
        in_specs += [
            pl.BlockSpec(left.shape, lambda i, source_ref, goes_ref: (0, 0)),
            pl.BlockSpec((1,) + paired[1].shape[1:], lambda i, source_ref, goes_ref: (i, 0, 0)),
        ]
        operands += list(paired)
    return pl.pallas_call(
        kernel,
        grid_spec=pltpu.PrefetchScalarGridSpec(
            num_scalar_prefetch=2,
            grid=(len(rels),),
            in_specs=in_specs,
            out_specs=[out_spec(c, size) for c, (_, size) in enumerate(cuts)],
        ),
        out_shape=[jax.ShapeDtypeStruct((len(rels), rank, size), jnp.bfloat16) for _, size in cuts],
        compiler_params=pltpu.CompilerParams(vmem_limit_bytes=24 * megabyte),
        cost_estimate=pl.CostEstimate(flops=4 * 10**9, bytes_accessed=25 * 10**6, transcendentals=0),
        name="partials",
    )(source, goes, *operands)


def correct(weights, gradient, halves, cuts, half_orders, last_bits):
    count = lax.axis_size("dp")
    me = lax.axis_index("dp")
    width = gradient.shape[1]
    rank = weights.shape[0]
    depth = gradient.shape[0] // count
    source = jnp.arange(count, dtype=jnp.int32) ^ me
    position = jnp.asarray(
        [[order.index(i & ~bit) for i in range(count)] for order, bit in zip(half_orders, last_bits)], jnp.int32
    )

    def kernel(source_ref, position_ref, weights_ref, gradient_ref, *refs):
        out_ref = refs[-1]
        step = pl.program_id(0)
        for c, ((start, size), bit) in enumerate(zip(cuts, last_bits)):
            rows = pl.ds(start, size)
            factor = jnp.where((step & bit) == 0, refs[2 * c][0], refs[2 * c + 1][0])
            term = jnp.dot(factor, weights_ref[...], preferred_element_type=jnp.float32)
            out_ref[rows, :] = (gradient_ref[rows, :].astype(jnp.float32) - term).astype(out_ref.dtype)

    def half_spec(c, size):
        return pl.BlockSpec((1, size, rank), lambda i, source_ref, position_ref: (position_ref[c, i], 0, 0))

    block = pl.BlockSpec((depth, width), lambda i, source_ref, position_ref: (source_ref[i], 0))
    return pl.pallas_call(
        kernel,
        grid_spec=pltpu.PrefetchScalarGridSpec(
            num_scalar_prefetch=2,
            grid=(count,),
            in_specs=[pl.BlockSpec((rank, width), lambda i, source_ref, position_ref: (0, 0)), block]
            + [half_spec(c, size) for c, (_, size) in enumerate(cuts) for _ in range(2)],
            out_specs=block,
        ),
        out_shape=jax.ShapeDtypeStruct(gradient.shape, gradient.dtype),
        compiler_params=pltpu.CompilerParams(vmem_limit_bytes=40 * megabyte),
        cost_estimate=pl.CostEstimate(flops=7 * 10**9, bytes_accessed=80 * 10**6, transcendentals=0),
        name="correct",
    )(source, position, weights, gradient, *halves)


def cut(extent, shares):
    unit = extent // sum(shares)
    out, start = [], 0
    for i, share in enumerate(shares):
        size = unit * share if i + 1 < len(shares) else extent - start
        out.append((start, size))
        start += size
    return out


def local(activations, test_matrix, gradient):
    count = lax.axis_size("dp")
    me = lax.axis_index("dp")
    own, hidden = activations.shape
    tokens = own * count
    probes = test_matrix.shape[1]
    rank = probes * count
    depth = hidden // count
    width = gradient.shape[1]
    bx, by, bl = 1, 2, 4
    lead = [1 << i for i in range(3, count.bit_length() - 1)][::-1]
    every = list(range(count))
    rotations = ((bx, by, bl), (by, bl, bx), (bl, bx, by))

    parts = cut(depth, (3, 3, 2, 2, 3))
    without = [[r for r in every if not r & bit] for bit in (bx, by)]
    with_bit = [[r | bit for r in rs] for rs, bit in zip(without, (bx, by))]

    give = [chosen(activations, depth, rels, *part) for rels, part in zip(with_bit, parts[:2])]
    probe_rows = test_matrix.T
    swapped = [across(value, bit) for value, bit in zip(give, (bx, by))]
    for bit in lead:
        probe_rows = jnp.concatenate([probe_rows, across(probe_rows, bit)], axis=0)
    probe_rows, *swapped = round_end(probe_rows, *swapped)
    strips = cut(hidden, (69, 69, 70))
    held = [probe_rows[:, start : start + size] for start, size in strips]
    for step in (0, 1):
        arrived = [across(value, order[step]) for value, order in zip(held, rotations)]
        held = [jnp.concatenate([a, b], axis=0) for a, b in zip(held, arrived)]
        held = round_end(*held)
    arrived = [across(value, order[2]) for value, order in zip(held, rotations)]

    def sketch_of(rows):
        return [
            low_mul(activations[:, start : start + size], value, ((1,), (1,)))
            for value, (start, size) in zip(rows, strips)
        ]

    early = sketch_of(held)
    gradient_blocks = gradient.reshape(count, depth, width)
    arrived = round_end(*arrived, *early)
    early, arrived = arrived[3:], arrived[:3]
    late = sketch_of(arrived)
    sketch = 0.0
    for order, first, second in zip(rotations, early, late):
        source = jnp.asarray(places(lead + list(order)), jnp.int32) ^ me
        columns = jnp.repeat(source, probes) * probes + jnp.tile(jnp.arange(probes), count)
        spread = (columns[:, None] == jnp.arange(rank)).astype(jnp.float32)
        sketch = sketch + mul(jnp.concatenate([first, second], axis=1), spread)
    sketch = total_tensor(sketch)
    sketch_low = sketch.astype(jnp.bfloat16)
    left = sketch_low.T

    orders = [lead + [bl, by], lead + [bl, bx], lead + [bl, by, bx], lead + [bl, bx, by], lead + [by, bx, bl]]
    places_of = [places(order) for order in orders]
    other_left = [across(left, bit) for bit in (bx, by)]
    pieces = list(partials(left, activations, depth, every, parts[2:], places_of[2:]))
    for i, bit in enumerate((bx, by)):
        slot = [without[i].index(r) for r in places_of[i]]
        pieces[i:i] = partials(
            left, activations, depth, without[i], parts[i : i + 1], [slot], (other_left[i], swapped[i])
        )
    core = mul(sketch, sketch_low.astype(jnp.float32), ((0,), (0,)))
    steps = [list(reversed(order)) for order in orders]
    turn = 0
    while any(steps):
        pieces = [send_half(piece, step.pop(0)) if step else piece for piece, step in zip(pieces, steps)]
        if turn == 0:
            for bit in [bx, by, bl] + lead:
                core = core + across(core, bit)
        turn += 1
        if any(steps):
            *pieces, core = round_end(*pieces, core)
    core = core / tokens
    core = 0.5 * (core + core.T)
    columns = jnp.concatenate([piece[0].astype(jnp.float32) for piece in pieces], axis=1) / tokens
    moment = mul(columns, columns, ((1,), (1,)))
    rows = columns.astype(jnp.bfloat16).T[None]
    rows, moment, core = round_end(rows, moment, core)

    for bit in lead:
        rows = jnp.concatenate([rows, across(rows, bit)], axis=0)
    for bit in [bx, by, bl] + lead:
        moment = moment + across(moment, bit)
    moment = total_tensor(moment)
    shares = cut(depth, (4, 4, 5))
    half_orders = [places(lead + list(order[:2])) for order in rotations]

    def facing(c, with_last):
        start, size = shares[c]
        source = jnp.asarray([r ^ (rotations[c][2] if with_last else 0) for r in half_orders[c]], jnp.int32) ^ me
        return jnp.take(gradient_blocks[:, start : start + size], source, axis=0)

    near = [facing(c, False) for c in range(3)]
    rows, moment, core, *near = round_end(rows, moment, core, *near)
    held = [rows[:, start : start + size] for start, size in shares]
    arrived = [across(value, order[0]) for value, order in zip(held, rotations)]
    held = [jnp.concatenate([a, b], axis=0) for a, b in zip(held, arrived)]
    *held, moment, core = round_end(*held, moment, core)
    arrived = [across(value, order[1]) for value, order in zip(held, rotations)]
    inverse = lower_inverse(core)
    held = [jnp.concatenate([a, b], axis=0) for a, b in zip(held, arrived)]
    *held, moment, inverse = round_end(*held, moment, inverse)
    arrived = [across(value, order[2]) for value, order in zip(held, rotations)]
    gram = mul(mul(inverse, moment), inverse, ((1,), (1,)))
    damping = damping_ratio * jnp.trace(gram) / rank
    step = mul(lower_inverse(gram + damping * jnp.eye(rank, dtype=jnp.float32)), inverse)
    solver = mul(step, step, ((0,), (0,)))

    def project(factors, facings):
        total = 0.0
        for factor, value in zip(factors, facings):
            total = total + low_mul(factor.reshape(-1, rank), value.reshape(-1, width), ((0,), (0,)))
        return total

    projected = project(held, near)
    far = [facing(c, True) for c in range(3)]
    ended = round_end(*arrived, *far, *held, solver, projected, gram)
    arrived, far, held = ended[:3], ended[3:6], ended[6:9]
    solver, projected, gram = ended[9:]
    projected = total_tensor(projected + project(arrived, far))
    weights = mul(solver, projected).astype(jnp.bfloat16)
    halves = [value for pair in zip(held, arrived) for value in pair]
    out = correct(weights, gradient, halves, shares, half_orders, [order[2] for order in rotations])
    return out, gram


def solution(mesh):
    placed = (P("dp", "tensor"), P("tensor", "dp"), P("tensor", "dp"))
    return jax.shard_map(
        local, mesh=mesh, in_specs=placed, out_specs=(P("tensor", "dp"), P()), check_vma=False
    )
```

time: 1030 us -> 585 us (0.57)
  waiting for transfers between devices: 755 us -> 207 us
  Pallas kernels: 0 us -> 99.4 us
  other arithmetic: 116 us -> 55.2 us
  local copies, waits for them, and re-layouts: 46.8 us -> 102 us
  starting transfers between devices: 9.25 us -> 58 us
  matrix products: 79.2 us -> 51 us
  between operations: 17.8 us -> 2.77 us
    all_gather x3 -> x0, waiting for transfers between devices: 505 us -> none  [the longest x1 380 us: local(): probe_full = lax.all_gather(test_matrix, 'dp', axis=1, tiled=True)]
    psum x4 -> x0, waiting for transfers between devices: 249 us -> none  [the longest x1 122 us: local(): gram_matrix = lax.psum(local_gram, ('dp', 'tensor'))]
    ppermute x0 -> x53, waiting for transfers between devices: none -> 207 us  [the longest x50 203 us: across(): return lax.ppermute(value, 'dp', [(i, i ^ bit) for i in range(count)])]
    another operation x18 -> x0, other arithmetic: 108 us -> none  [the longest x7 34.6 us: local(): jnp.linalg.cholesky(gram_matrix + damping * jnp.eye(rank_size, dtype=jnp....]
    pallas_call x0 -> x8, Pallas kernels: none -> 99.4 us  [the longest x2 51.4 us: lower_inverse(): pl.pallas_call(lower_inverse_kernel, out_shape=jax.ShapeDtypeStruct(matri...]
    ppermute x0 -> x53, starting transfers between devices: none -> 58 us  [the longest x50 57.8 us: across(): return lax.ppermute(value, 'dp', [(i, i ^ bit) for i in range(count)])]
    gather x0 -> x6, local copies, waits for them, and re-layouts: none -> 39.5 us  [facing(): return jnp.take(gradient_blocks[:, start:start + size], source, axis=0)]
    slice x0 -> x24, local copies, waits for them, and re-layouts: none -> 31.4 us  [the longest x2 20.4 us: facing(): return jnp.take(gradient_blocks[:, start:start + size], source, axis=0)]
  transfers between devices with their start and end apart: 8 -> 53, of which waited for: 6 -> 33; matrix products, arithmetic and copies ran while one was open for 18% -> 27% of each run, Pallas kernels for 0% -> 12%
where the time goes in v1:
time: 585 us; the launch traced here: 575 us
  waiting for transfers between devices  207 us (35%)
  local copies, waits for them, and re-layouts  102 us (17%)
  Pallas kernels  99.4 us (17%)
  starting transfers between devices  58 us (10%)
  other arithmetic  55.2 us (9%)
  matrix products  51 us (9%)
    ppermute x50, waiting for transfers between devices, across(): return lax.ppermute(value, 'dp', [(i, i ^ bit) for i in range(count)])  203 us
    ppermute x50, starting transfers between devices, across(): return lax.ppermute(value, 'dp', [(i, i ^ bit) for i in range(count)])  57.8 us
    pallas_call x2, Pallas kernels, lower_inverse(): pl.pallas_call(lower_inverse_kernel, out_shape=jax.ShapeDtypeStruct(matri...  51.4 us
    dot_general x12, matrix products, low_mul(): lax.dot_general(a, b, (dims, ((), ())), preferred_element_type=jnp.float32)  43.3 us
    gather x6, local copies, waits for them, and re-layouts, facing(): return jnp.take(gradient_blocks[:, start:start + size], source, axis=0)  39.5 us
    pallas_call x1, Pallas kernels, correct(): pl.pallas_call(kernel, grid_spec=pltpu.PrefetchScalarGridSpec(num_scalar_...  31.1 us
    select_n x6, other arithmetic, facing(): return jnp.take(gradient_blocks[:, start:start + size], source, axis=0)  25.2 us
    unnamed x100, local copies, waits for them, and re-layouts  21.3 us
  transfers between devices with their start and end apart: 53, of which 33 were waited for; matrix products, arithmetic and copies ran while one was open for 27% of the time, Pallas kernels for 12%

profile of v1, /device:TPU:0, one launch (start us, length us, event | category | flops | bytes accessed | tf_op | source)
XLA Modules:
  0.0 575.1 jit_solution(13806365391345087380)
XLA Ops:
  5.4 4.9 copy-done
  16.3 25.8 %collective-permute-done = bf16[16,26624]{1,0:T(8,128)(2,1)S(1)} collective-permute-done((bf16[16,26624]{1,0:T(8,128)(2,1)}, bf16[16,26624]{1,0:T(8,128)(2,1)S(1)}, u32[]{:S(2)}, u32[]{:S(2)}) %collective-permute-start) | collective-permute-done | bytes 852000 | tf_op jit(solution)/shard_map/ppermute | solution.py:23
  42.3 5.4 collective-permute-done.1.refs_1_
  54.3 9.3 %collective-permute-done.4 = bf16[32,8832]{1,0:T(8,128)(2,1)S(1)} collective-permute-done((bf16[32,8832]{1,0:T(8,128)(2,1)S(1)}, bf16[32,8832]{1,0:T(8,128)(2,1)S(1)}, u32[]{:S(2)}, u32[]{:S(2)}) %collective-permute-start.4) | collective-permute-done | bytes 565280 | tf_op jit(solution)/shard_map/ppermute | solution.py:23
  69.1 20.0 %collective-permute-done.6 = bf16[64,8832]{1,0:T(8,128)(2,1)S(1)} collective-permute-done((bf16[64,8832]{1,0:T(8,128)(2,1)S(1)}, bf16[64,8832]{1,0:T(8,128)(2,1)S(1)}, u32[]{:S(2)}, u32[]{:S(2)}) %collective-permute-start.6) | collective-permute-done | bytes 1130528 | tf_op jit(solution)/shard_map/ppermute | solution.py:23
  107.3 4.8 fusion.30
  112.0 29.1 %collective-permute-done.9 = bf16[128,8832]{1,0:T(8,128)(2,1)} collective-permute-done((bf16[128,8832]{1,0:T(8,128)(2,1)}, bf16[128,8832]{1,0:T(8,128)(2,1)}, u32[]{:S(2)}, u32[]{:S(2)}) %collective-permute-start.9) | collective-permute-done | bytes 2261024 | tf_op jit(solution)/shard_map/ppermute | solution.py:23
  170.1 4.9 copy-done.1
  184.3 4.9 copy-done.2
  189.2 6.7 %partials.5 = (bf16[16,256,256]{2,1,0:T(8,128)(2,1)S(1)}, bf16[16,256,256]{2,1,0:T(8,128)(2,1)S(1)}, bf16[16,256,384]{2,1,0:T(8,128)(2,1)S(1)}) custom-call(s32[16]{0:T(128)S(1)} %iota_xor_fusion.source_ref, s32[3,16]{1,0:T(4,128)S(1)} %copy-done.10, bf16[256,256]{1,0:T(8,128)(2,1)S(1)} %convert_bitcast_fusion.left_ref, bf16[256,26624]{1,0:T(8,128)(2,1)S(1)} %copy-done.2), custom_call_target="tpu_custom_call" | custom-call | flops 4000000000 | bytes 25000000 | tf_op jit(solution)/shard_map/partials/pallas_call | solution.py:160
  229.0 12.7 %collective-permute-done.18 = bf16[8,256,256]{1,2,0:T(8,128)(2,1)} collective-permute-done((bf16[8,256,256]{1,2,0:T(8,128)(2,1)}, bf16[8,256,256]{1,2,0:T(8,128)(2,1)}, u32[]{:S(2)}, u32[]{:S(2)}) %collective-permute-start.18) | collective-permute-done | bytes 1048608 | tf_op jit(solution)/shard_map/ppermute | solution.py:23
  243.2 8.2 %collective-permute-done.23 = f32[256,256]{0,1:T(8,128)S(1)} collective-permute-done((f32[256,256]{0,1:T(8,128)S(1)}, f32[256,256]{0,1:T(8,128)S(1)}, u32[]{:S(2)}, u32[]{:S(2)}) %collective-permute-start.23) | collective-permute-done | bytes 262176 | tf_op jit(solution)/shard_map/ppermute | solution.py:23
  257.8 11.4 %fusion.66 = (bf16[16,512,512]{2,1,0:T(8,128)(2,1)}, bf16[16,512,512]{2,1,0:T(8,128)(2,1)}) fusion(bf16[16,1664,512]{2,1,0:T(8,128)(2,1)} %bitcast.89), kind=kLoop, calls=%fused_computation.148 | loop fusion | bytes 33554432 | tf_op jit(solution)/shard_map/slice | solution.py:316
  272.7 5.8 %collective-permute-done.26 = bf16[4,256,256]{1,2,0:T(8,128)(2,1)S(1)} collective-permute-done((bf16[4,256,256]{1,2,0:T(8,128)(2,1)S(1)}, bf16[4,256,256]{1,2,0:T(8,128)(2,1)S(1)}, u32[]{:S(2)}, u32[]{:S(2)}) %collective-permute-start.26) | collective-permute-done | bytes 524320 | tf_op jit(solution)/shard_map/ppermute | solution.py:23
  278.7 6.7 %collective-permute-done.28 = bf16[4,256,384]{1,2,0:T(8,128)(2,1)S(1)} collective-permute-done((bf16[4,256,384]{1,2,0:T(8,128)(2,1)S(1)}, bf16[4,256,384]{1,2,0:T(8,128)(2,1)S(1)}, u32[]{:S(2)}, u32[]{:S(2)}) %collective-permute-start.28) | collective-permute-done | bytes 786464 | tf_op jit(solution)/shard_map/ppermute | solution.py:23
  286.5 9.0 %slice.222 = bf16[16,640,512]{2,1,0:T(8,128)(2,1)} slice(bf16[16,1664,512]{2,1,0:T(8,128)(2,1)} %bitcast.90), slice={[0:16], [1024:1664], [0:512]} | slice | bytes 20971520 | tf_op jit(solution)/shard_map/slice | solution.py:316
  295.5 7.2 %gather_fusion.2 = bf16[8,640,512]{2,1,0:T(8,128)(2,1)} fusion(bf16[16,640,512]{2,1,0:T(8,128)(2,1)} %slice.222, s32[1024]{0:T(1024)S(1)} %pad_clamp_fusion.3), kind=kCustom, calls=%fused_computation.1.clone | custom fusion | bytes 10485792 | tf_op jit(solution)/shard_map/jit(_take)/gather | solution.py:316
  322.4 8.6 %collective-permute-done.34 = bf16[1,256,256]{1,2,0:T(8,128)(2,1)S(1)} collective-permute-done((bf16[1,256,256]{1,2,0:T(8,128)(2,1)S(1)}, bf16[1,256,256]{1,2,0:T(8,128)(2,1)S(1)}, u32[]{:S(2)}, u32[]{:S(2)}) %collective-permute-start.34) | collective-permute-done | bytes 131104 | tf_op jit(solution)/shard_map/ppermute | solution.py:23
  337.9 6.3 %gather_fusion.1 = bf16[8,512,512]{2,1,0:T(8,128)(2,1)} fusion(bf16[16,512,512]{2,1,0:T(8,128)(2,1)} %get-tuple-element.150, s32[1024]{0:T(1024)S(1)} %pad_clamp_fusion.4), kind=kCustom, calls=%fused_computation.2.clone | custom fusion | bytes 8388640 | tf_op jit(solution)/shard_map/jit(_take)/gather | solution.py:316
  345.0 5.6 broadcast_select_fusion.1
  354.8 6.2 %gather_fusion = bf16[8,512,512]{2,1,0:T(8,128)(2,1)} fusion(bf16[16,512,512]{2,1,0:T(8,128)(2,1)} %get-tuple-element.151, s32[1024]{0:T(1024)S(1)} %pad_clamp_fusion.5), kind=kCustom, calls=%fused_computation.clone | custom fusion | bytes 8388640 | tf_op jit(solution)/shard_map/jit(_take)/gather | solution.py:316
  360.9 5.7 collective-permute-done.40
  373.2 14.6 %collective-permute-done.41 = f32[256,256]{1,0:T(8,128)S(1)} collective-permute-done((f32[256,256]{1,0:T(8,128)S(1)}, f32[256,256]{1,0:T(8,128)S(1)}, u32[]{:S(2)}, u32[]{:S(2)}) %collective-permute-start.41) | collective-permute-done | bytes 262176 | tf_op jit(solution)/shard_map/ppermute | solution.py:23
  391.8 6.3 %gather_fusion.4 = bf16[8,512,512]{2,1,0:T(8,128)(2,1)} fusion(bf16[16,512,512]{2,1,0:T(8,128)(2,1)} %get-tuple-element.150, s32[1024]{0:T(1024)S(1)} %pad_clamp_fusion.1), kind=kCustom, calls=%fused_computation.4.clone | custom fusion | bytes 8388640 | tf_op jit(solution)/shard_map/jit(_take)/gather | solution.py:316
  406.1 5.9 %collective-permute-done.43 = bf16[2,512,256]{2,1,0:T(8,128)(2,1)S(1)} collective-permute-done((bf16[2,512,256]{2,1,0:T(8,128)(2,1)S(1)}, bf16[2,512,256]{2,1,0:T(8,128)(2,1)S(1)}, u32[]{:S(2)}, u32[]{:S(2)}) %collective-permute-start.43) | collective-permute-done | bytes 524320 | tf_op jit(solution)/shard_map/ppermute | solution.py:23
  418.3 7.2 %gather_fusion.5 = bf16[8,640,512]{2,1,0:T(8,128)(2,1)} fusion(bf16[16,640,512]{2,1,0:T(8,128)(2,1)} %slice.222, s32[1024]{0:T(1024)S(1)} %pad_clamp_fusion), kind=kCustom, calls=%fused_computation.5.clone | custom fusion | bytes 10485792 | tf_op jit(solution)/shard_map/jit(_take)/gather | solution.py:316
  425.6 6.4 %gather_fusion.3 = bf16[8,512,512]{2,1,0:T(8,128)(2,1)} fusion(bf16[16,512,512]{2,1,0:T(8,128)(2,1)} %get-tuple-element.151, s32[1024]{0:T(1024)S(1)} %pad_clamp_fusion.2), kind=kCustom, calls=%fused_computation.3.clone | custom fusion | bytes 8388640 | tf_op jit(solution)/shard_map/jit(_take)/gather | solution.py:316
  432.2 4.8 broadcast_select_fusion.3
  440.0 25.6 %lower_inverse.2 = f32[256,256]{1,0:T(8,128)S(1)} custom-call(f32[256,256]{1,0:T(8,128)S(1)} %fusion.49.matrix_ref), custom_call_target="tpu_custom_call" | custom-call | flops 100000000 | bytes 1000000 | tf_op jit(solution)/shard_map/lower_inverse/pallas_call | solution.py:83
  478.3 25.8 %lower_inverse.3 = f32[256,256]{1,0:T(8,128)S(1)} custom-call(f32[256,256]{1,0:T(8,128)S(1)} %select_add_fusion.matrix_ref), custom_call_target="tpu_custom_call" | custom-call | flops 100000000 | bytes 1000000 | tf_op jit(solution)/shard_map/lower_inverse/pallas_call | solution.py:83
  519.5 11.8 %collective-permute-done.51.refs_5_ = bf16[8,640,256]{2,1,0:T(8,128)(2,1)} collective-permute-done((bf16[8,640,256]{2,1,0:T(8,128)(2,1)}, bf16[8,640,256]{2,1,0:T(8,128)(2,1)}, u32[]{:S(2)}, u32[]{:S(2)}) %collective-permute-start.51) | collective-permute-done | bytes 2621472 | tf_op jit(solution)/shard_map/ppermute | solution.py:23
  543.5 31.1 %correct.1 = bf16[26624,512]{1,0:T(8,128)(2,1)} custom-call(s32[16]{0:T(128)S(1)} %iota_xor_fusion.source_ref, s32[3,16]{1,0:T(4,128)S(1)} %copy-done.8, bf16[256,512]{1,0:T(8,128)(2,1)S(1)} %convolution_convert_fusion.weights_ref, bf16[26624,512]{1,0:T(8,128)(2,1)} %gradient_ref.1, bf16[8,512,256]{2,1,0:T(8,128)(2,1)} %pad_maximum_fusion.4.refs_0_, ...), custom_call_target="tpu_custom_call" | custom-call | flops 7000000000 | bytes 80000000 | tf_op jit(solution)/shard_map/correct/pallas_call | solution.py:199
  (316 shorter events, 223.8 us)
Async XLA Ops:
  0.6 41.5 %collective-permute-start = (bf16[16,26624]{1,0:T(8,128)(2,1)}, bf16[16,26624]{1,0:T(8,128)(2,1)S(1)}, u32[]{:S(2)}, u32[]{:S(2)}) collective-permute-start(bf16[16,26624]{1,0:T(8,128)(2,1)} %bitcast.95), channel_id=1, source_target_pairs={{0,16},{2,18},{4,20},{6,22},{8,24},{10,26},{12,28},{14,30},{16,0},... | collective-permute-start | bytes 2555912 | tf_op jit(solution)/shard_map/ppermute | solution.py:23
  11.7 35.9 %collective-permute-start.1 = (bf16[8,256,384]{2,1,0:T(8,128)(2,1)S(1)}, bf16[8,256,384]{2,1,0:T(8,128)(2,1)S(1)}, u32[]{:S(2)}, u32[]{:S(2)}) collective-permute-start(bf16[8,256,384]{2,1,0:T(8,128)(2,1)S(1)} %chosen.2), channel_id=1, source_target_pairs={{0,2},{2,0},{4,6},{6,4},{8,10},{10,8},{12,14},{14,12},{16,18},{18,... | collective-permute-start | bytes 4718600 | tf_op jit(solution)/shard_map/ppermute | solution.py:23
  14.7 35.6 %collective-permute-start.2 = (bf16[8,256,384]{2,1,0:T(8,128)(2,1)S(1)}, bf16[8,256,384]{2,1,0:T(8,128)(2,1)S(1)}, u32[]{:S(2)}, u32[]{:S(2)}) collective-permute-start(bf16[8,256,384]{2,1,0:T(8,128)(2,1)S(1)} %chosen.3), channel_id=1, source_target_pairs={{0,4},{2,6},{4,0},{6,2},{8,12},{10,14},{12,8},{14,10},{16,20},{18,... | collective-permute-start | bytes 4718600 | tf_op jit(solution)/shard_map/ppermute | solution.py:23
  65.5 23.7 %collective-permute-start.6 = (bf16[64,8832]{1,0:T(8,128)(2,1)S(1)}, bf16[64,8832]{1,0:T(8,128)(2,1)S(1)}, u32[]{:S(2)}, u32[]{:S(2)}) collective-permute-start(bf16[64,8832]{1,0:T(8,128)(2,1)S(1)} %pad_maximum_fusion.10), channel_id=1, source_target_pairs={{0,4},{2,6},{4,0},{6,2},{8,12},{10,14},{12,8},{14,10},{16,20},{18,... | collective-permute-start | bytes 3391496 | tf_op jit(solution)/shard_map/ppermute | solution.py:23
  66.0 24.7 %collective-permute-start.7 = (bf16[64,8832]{1,0:T(8,128)(2,1)S(1)}, bf16[64,8832]{1,0:T(8,128)(2,1)S(1)}, u32[]{:S(2)}, u32[]{:S(2)}) collective-permute-start(bf16[64,8832]{1,0:T(8,128)(2,1)S(1)} %pad_maximum_fusion.11), channel_id=1, source_target_pairs={{0,8},{2,10},{4,12},{6,14},{8,0},{10,2},{12,4},{14,6},{16,24},{18,... | collective-permute-start | bytes 3391496 | tf_op jit(solution)/shard_map/ppermute | solution.py:23
  67.6 24.7 %collective-permute-start.8 = (bf16[64,8960]{1,0:T(8,128)(2,1)S(1)}, bf16[64,8960]{1,0:T(8,128)(2,1)S(1)}, u32[]{:S(2)}, u32[]{:S(2)}) collective-permute-start(bf16[64,8960]{1,0:T(8,128)(2,1)S(1)} %pad_maximum_fusion.9), channel_id=1, source_target_pairs={{0,2},{2,0},{4,6},{6,4},{8,10},{10,8},{12,14},{14,12},{16,18},{18,... | collective-permute-start | bytes 3440648 | tf_op jit(solution)/shard_map/ppermute | solution.py:23
  93.9 47.3 %collective-permute-start.9 = (bf16[128,8832]{1,0:T(8,128)(2,1)}, bf16[128,8832]{1,0:T(8,128)(2,1)}, u32[]{:S(2)}, u32[]{:S(2)}) collective-permute-start(bf16[128,8832]{1,0:T(8,128)(2,1)} %pad_maximum_fusion.2), channel_id=1, source_target_pairs={{0,8},{2,10},{4,12},{6,14},{8,0},{10,2},{12,4},{14,6},{16,24},{18,... | collective-permute-start | bytes 6782984 | tf_op jit(solution)/shard_map/ppermute | solution.py:23
  95.4 47.0 %collective-permute-start.10 = (bf16[128,8832]{1,0:T(8,128)(2,1)}, bf16[128,8832]{1,0:T(8,128)(2,1)}, u32[]{:S(2)}, u32[]{:S(2)}) collective-permute-start(bf16[128,8832]{1,0:T(8,128)(2,1)} %pad_maximum_fusion.3), channel_id=1, source_target_pairs={{0,2},{2,0},{4,6},{6,4},{8,10},{10,8},{12,14},{14,12},{16,18},{18,... | collective-permute-start | bytes 6782984 | tf_op jit(solution)/shard_map/ppermute | solution.py:23
  96.9 47.4 %collective-permute-start.11 = (bf16[128,8960]{1,0:T(8,128)(2,1)}, bf16[128,8960]{1,0:T(8,128)(2,1)}, u32[]{:S(2)}, u32[]{:S(2)}) collective-permute-start(bf16[128,8960]{1,0:T(8,128)(2,1)} %pad_maximum_fusion.1), channel_id=1, source_target_pairs={{0,4},{2,6},{4,0},{6,2},{8,12},{10,14},{12,8},{14,10},{16,20},{18,... | collective-permute-start | bytes 6881288 | tf_op jit(solution)/shard_map/ppermute | solution.py:23
  158.8 24.1 %collective-permute-start.20 = (f32[256,256]{0,1:T(8,128)S(1)}, f32[256,256]{0,1:T(8,128)S(1)}, u32[]{:S(2)}, u32[]{:S(2)}) collective-permute-start(f32[256,256]{0,1:T(8,128)S(1)} %fusion.52), channel_id=1, source_target_pairs={{0,2},{2,0},{4,6},{6,4},{8,10},{10,8},{12,14},{14,12},{16,18},{18,... | collective-permute-start | bytes 786440 | tf_op jit(solution)/shard_map/ppermute | solution.py:23
  180.9 43.1 %collective-permute-start.16 = (bf16[4,256,384]{1,2,0:T(8,128)(2,1)}, bf16[4,256,384]{1,2,0:T(8,128)(2,1)}, u32[]{:S(2)}, u32[]{:S(2)}) collective-permute-start(bf16[4,256,384]{1,2,0:T(8,128)(2,1)} %copy.58), channel_id=1, source_target_pairs={{0,2},{2,0},{4,6},{6,4},{8,10},{10,8},{12,14},{14,12},{16,18},{18,... | collective-permute-start | bytes 2359304 | tf_op jit(solution)/shard_map/ppermute | solution.py:23
  181.5 44.4 %collective-permute-start.14 = (bf16[4,256,384]{1,2,0:T(8,128)(2,1)}, bf16[4,256,384]{1,2,0:T(8,128)(2,1)}, u32[]{:S(2)}, u32[]{:S(2)}) collective-permute-start(bf16[4,256,384]{1,2,0:T(8,128)(2,1)} %copy.56), channel_id=1, source_target_pairs={{0,4},{2,6},{4,0},{6,2},{8,12},{10,14},{12,8},{14,10},{16,20},{18,... | collective-permute-start | bytes 2359304 | tf_op jit(solution)/shard_map/ppermute | solution.py:23
  183.6 22.5 %collective-permute-start.21 = (f32[256,256]{0,1:T(8,128)}, f32[256,256]{0,1:T(8,128)}, u32[]{:S(2)}, u32[]{:S(2)}) collective-permute-start(f32[256,256]{0,1:T(8,128)} %add.164), channel_id=1, source_target_pairs={{0,4},{2,6},{4,0},{6,2},{8,12},{10,14},{12,8},{14,10},{16,20},{18,... | collective-permute-start | bytes 786440 | tf_op jit(solution)/shard_map/ppermute | solution.py:23
  204.7 22.7 %collective-permute-start.17 = (bf16[8,256,256]{1,2,0:T(8,128)(2,1)}, bf16[8,256,256]{1,2,0:T(8,128)(2,1)}, u32[]{:S(2)}, u32[]{:S(2)}) collective-permute-start(bf16[8,256,256]{1,2,0:T(8,128)(2,1)} %slice.215), channel_id=1, source_target_pairs={{0,2},{2,0},{4,6},{6,4},{8,10},{10,8},{12,14},{14,12},{16,18},{18,... | collective-permute-start | bytes 3145736 | tf_op jit(solution)/shard_map/ppermute | solution.py:23
  213.7 39.3 %collective-permute-start.19 = (bf16[8,256,384]{1,2,0:T(8,128)(2,1)}, bf16[8,256,384]{1,2,0:T(8,128)(2,1)}, u32[]{:S(2)}, u32[]{:S(2)}) collective-permute-start(bf16[8,256,384]{1,2,0:T(8,128)(2,1)} %slice.219), channel_id=1, source_target_pairs={{0,8},{2,10},{4,12},{6,14},{8,0},{10,2},{12,4},{14,6},{16,24},{18,... | collective-permute-start | bytes 4718600 | tf_op jit(solution)/shard_map/ppermute | solution.py:23
  220.1 21.6 %collective-permute-start.18 = (bf16[8,256,256]{1,2,0:T(8,128)(2,1)}, bf16[8,256,256]{1,2,0:T(8,128)(2,1)}, u32[]{:S(2)}, u32[]{:S(2)}) collective-permute-start(bf16[8,256,256]{1,2,0:T(8,128)(2,1)} %slice.217), channel_id=1, source_target_pairs={{0,4},{2,6},{4,0},{6,2},{8,12},{10,14},{12,8},{14,10},{16,20},{18,... | collective-permute-start | bytes 3145736 | tf_op jit(solution)/shard_map/ppermute | solution.py:23
  224.0 27.4 %collective-permute-start.23 = (f32[256,256]{0,1:T(8,128)S(1)}, f32[256,256]{0,1:T(8,128)S(1)}, u32[]{:S(2)}, u32[]{:S(2)}) collective-permute-start(f32[256,256]{0,1:T(8,128)S(1)} %add.166), channel_id=1, source_target_pairs={{0,16},{2,18},{4,20},{6,22},{8,24},{10,26},{12,28},{14,30},{16,0},... | collective-permute-start | bytes 786440 | tf_op jit(solution)/shard_map/ppermute | solution.py:23
  255.0 17.3 %collective-permute-start.25 = (bf16[2,256,384]{1,2,0:T(8,128)(2,1)S(1)}, bf16[2,256,384]{1,2,0:T(8,128)(2,1)S(1)}, u32[]{:S(2)}, u32[]{:S(2)}) collective-permute-start(bf16[2,256,384]{1,2,0:T(8,128)(2,1)S(1)} %slice.169), channel_id=1, source_target_pairs={{0,8},{2,10},{4,12},{6,14},{8,0},{10,2},{12,4},{14,6},{16,24},{18,... | collective-permute-start | bytes 1179656 | tf_op jit(solution)/shard_map/ppermute | solution.py:23
  255.3 17.1 %collective-permute-start.24 = (bf16[2,256,384]{1,2,0:T(8,128)(2,1)S(1)}, bf16[2,256,384]{1,2,0:T(8,128)(2,1)S(1)}, u32[]{:S(2)}, u32[]{:S(2)}) collective-permute-start(bf16[2,256,384]{1,2,0:T(8,128)(2,1)S(1)} %slice.167), channel_id=1, source_target_pairs={{0,8},{2,10},{4,12},{6,14},{8,0},{10,2},{12,4},{14,6},{16,24},{18,... | collective-permute-start | bytes 1179656 | tf_op jit(solution)/shard_map/ppermute | solution.py:23
  257.1 15.4 %collective-permute-start.27 = (bf16[4,256,256]{1,2,0:T(8,128)(2,1)S(1)}, bf16[4,256,256]{1,2,0:T(8,128)(2,1)S(1)}, u32[]{:S(2)}, u32[]{:S(2)}) collective-permute-start(bf16[4,256,256]{1,2,0:T(8,128)(2,1)S(1)} %slice.173), channel_id=1, source_target_pairs={{0,2},{2,0},{4,6},{6,4},{8,10},{10,8},{12,14},{14,12},{16,18},{18,... | collective-permute-start | bytes 1572872 | tf_op jit(solution)/shard_map/ppermute | solution.py:23
  270.8 14.6 %collective-permute-start.28 = (bf16[4,256,384]{1,2,0:T(8,128)(2,1)S(1)}, bf16[4,256,384]{1,2,0:T(8,128)(2,1)S(1)}, u32[]{:S(2)}, u32[]{:S(2)}) collective-permute-start(bf16[4,256,384]{1,2,0:T(8,128)(2,1)S(1)} %slice.175), channel_id=1, source_target_pairs={{0,2},{2,0},{4,6},{6,4},{8,10},{10,8},{12,14},{14,12},{16,18},{18,... | collective-permute-start | bytes 2359304 | tf_op jit(solution)/shard_map/ppermute | solution.py:23
  285.6 22.2 %collective-permute-start.30 = (bf16[1,256,384]{1,2,0:T(8,128)(2,1)S(1)}, bf16[1,256,384]{1,2,0:T(8,128)(2,1)S(1)}, u32[]{:S(2)}, u32[]{:S(2)}) collective-permute-start(bf16[1,256,384]{1,2,0:T(8,128)(2,1)S(1)} %slice.179), channel_id=1, source_target_pairs={{0,16},{2,18},{4,20},{6,22},{8,24},{10,26},{12,28},{14,30},{16,0},... | collective-permute-start | bytes 589832 | tf_op jit(solution)/shard_map/ppermute | solution.py:23
  350.5 37.4 %collective-permute-start.37 = (bf16[1,1664,256]{2,1,0:T(8,128)(2,1)S(1)}, bf16[1,1664,256]{2,1,0:T(8,128)(2,1)}, u32[]{:S(2)}, u32[]{:S(2)}) collective-permute-start(bf16[1,1664,256]{2,1,0:T(8,128)(2,1)S(1)} %fusion.36), channel_id=1, source_target_pairs={{0,16},{2,18},{4,20},{6,22},{8,24},{10,26},{12,28},{14,30},{16,0},... | collective-permute-start | bytes 2555912 | tf_op jit(solution)/shard_map/ppermute | solution.py:23
  350.7 15.9 %collective-permute-start.40 = (f32[256,256]{1,0:T(8,128)S(1)}, f32[256,256]{1,0:T(8,128)S(1)}, u32[]{:S(2)}, u32[]{:S(2)}) collective-permute-start(f32[256,256]{1,0:T(8,128)S(1)} %add.183), channel_id=1, source_target_pairs={{0,8},{2,10},{4,12},{6,14},{8,0},{10,2},{12,4},{14,6},{16,24},{18,... | collective-permute-start | bytes 786440 | tf_op jit(solution)/shard_map/ppermute | solution.py:23
  366.6 21.2 %collective-permute-start.41 = (f32[256,256]{1,0:T(8,128)S(1)}, f32[256,256]{1,0:T(8,128)S(1)}, u32[]{:S(2)}, u32[]{:S(2)}) collective-permute-start(f32[256,256]{1,0:T(8,128)S(1)} %add.184), channel_id=1, source_target_pairs={{0,16},{2,18},{4,20},{6,22},{8,24},{10,26},{12,28},{14,30},{16,0},... | collective-permute-start | bytes 786440 | tf_op jit(solution)/shard_map/ppermute | solution.py:23
  398.7 16.4 %collective-permute-start.45 = (bf16[2,640,256]{2,1,0:T(8,128)(2,1)S(1)}, bf16[2,640,256]{2,1,0:T(8,128)(2,1)S(1)}, u32[]{:S(2)}, u32[]{:S(2)}) collective-permute-start(bf16[2,640,256]{2,1,0:T(8,128)(2,1)S(1)} %slice.197), channel_id=1, source_target_pairs={{0,8},{2,10},{4,12},{6,14},{8,0},{10,2},{12,4},{14,6},{16,24},{18,... | collective-permute-start | bytes 1966088 | tf_op jit(solution)/shard_map/ppermute | solution.py:23
  416.3 49.3 %collective-permute-start.46 = (bf16[4,512,256]{2,1,0:T(8,128)(2,1)}, bf16[4,512,256]{2,1,0:T(8,128)(2,1)}, u32[]{:S(2)}, u32[]{:S(2)}) collective-permute-start(bf16[4,512,256]{2,1,0:T(8,128)(2,1)} %pad_maximum_fusion.12), channel_id=1, source_target_pairs={{0,4},{2,6},{4,0},{6,2},{8,12},{10,14},{12,8},{14,10},{16,20},{18,... | collective-permute-start | bytes 3145736 | tf_op jit(solution)/shard_map/ppermute | solution.py:23
  416.9 52.0 %collective-permute-start.48 = (bf16[4,640,256]{2,1,0:T(8,128)(2,1)}, bf16[4,640,256]{2,1,0:T(8,128)(2,1)}, u32[]{:S(2)}, u32[]{:S(2)}) collective-permute-start(bf16[4,640,256]{2,1,0:T(8,128)(2,1)} %pad_maximum_fusion.8), channel_id=1, source_target_pairs={{0,2},{2,0},{4,6},{6,4},{8,10},{10,8},{12,14},{14,12},{16,18},{18,... | collective-permute-start | bytes 3932168 | tf_op jit(solution)/shard_map/ppermute | solution.py:23
  432.0 36.8 %collective-permute-start.47 = (bf16[4,512,256]{2,1,0:T(8,128)(2,1)S(1)}, bf16[4,512,256]{2,1,0:T(8,128)(2,1)S(1)}, u32[]{:S(2)}, u32[]{:S(2)}) collective-permute-start(bf16[4,512,256]{2,1,0:T(8,128)(2,1)S(1)} %pad_maximum_fusion.13), channel_id=1, source_target_pairs={{0,8},{2,10},{4,12},{6,14},{8,0},{10,2},{12,4},{14,6},{16,24},{18,... | collective-permute-start | bytes 3145736 | tf_op jit(solution)/shard_map/ppermute | solution.py:23
  472.4 46.2 %collective-permute-start.49 = (bf16[8,512,256]{2,1,0:T(8,128)(2,1)}, bf16[8,512,256]{2,1,0:T(8,128)(2,1)}, u32[]{:S(2)}, u32[]{:S(2)}) collective-permute-start(bf16[8,512,256]{2,1,0:T(8,128)(2,1)} %pad_maximum_fusion.4.refs_0_), channel_id=1, source_target_pairs={{0,8},{2,10},{4,12},{6,14},{8,0},{10,2},{12,4},{14,6},{16,24},{18,... | collective-permute-start | bytes 6291464 | tf_op jit(solution)/shard_map/ppermute | solution.py:23
  474.2 45.4 %collective-permute-start.50 = (bf16[8,512,256]{2,1,0:T(8,128)(2,1)S(1)}, bf16[8,512,256]{2,1,0:T(8,128)(2,1)}, u32[]{:S(2)}, u32[]{:S(2)}) collective-permute-start(bf16[8,512,256]{2,1,0:T(8,128)(2,1)S(1)} %pad_maximum_fusion.5.refs_2_), channel_id=1, source_target_pairs={{0,2},{2,0},{4,6},{6,4},{8,10},{10,8},{12,14},{14,12},{16,18},{18,... | collective-permute-start | bytes 6291464 | tf_op jit(solution)/shard_map/ppermute | solution.py:23
  474.8 56.6 %collective-permute-start.51 = (bf16[8,640,256]{2,1,0:T(8,128)(2,1)}, bf16[8,640,256]{2,1,0:T(8,128)(2,1)}, u32[]{:S(2)}, u32[]{:S(2)}) collective-permute-start(bf16[8,640,256]{2,1,0:T(8,128)(2,1)} %pad_maximum_fusion.refs_4_), channel_id=1, source_target_pairs={{0,4},{2,6},{4,0},{6,2},{8,12},{10,14},{12,8},{14,10},{16,20},{18,... | collective-permute-start | bytes 7864328 | tf_op jit(solution)/shard_map/ppermute | solution.py:23
  (68 other events, 822.8 us)
